TPU v7x, 256 devices: a whole 4x4x8 slice. The times are simulated.
256 devices in a mesh: dp: 4 (over x_lo, core), center: 64 (over y, x_hi, z).
Axes of the slice: x: 4 (x_hi: 2, x_lo: 2; x = x_hi * 2 + x_lo), y: 4, z: 8, core: 2. Of those that a mesh axis runs over, the one named last changes fastest.
Arguments:
- centers: bfloat16 [131072, 768], P('center'), may hold values from -0.5 to 0.5
- weights: float32 [131072, 256], P('center'), may hold values from -0.0625 to 0.0625
- batch_index: int32 [1024], P('dp'), may hold values from 0 to 131071
- targets: float32 [1024, 256], P('dp'), may hold values from -6 to 6
- subset_points: bfloat16 [2048, 768], P('center'), may hold values from -0.5 to 0.5
- eigvecs: float32 [2048, 200], P('center'), may hold values from -0.125 to 0.125
- shrink: float32 [200], replicated, may hold values from 0.05 to 0.95
Outputs:
- step: float32 [131072, 256], P('center')
All inputs are finite; a program needn't handle non-finite values.
Results may differ from a plain program's by a relative error of at most 0.0003.
Values may be sent and summed in bfloat16 or wider, within the bound.
A program may use at most 128 MiB of HBM per device.

v0:
```python
import jax
import jax.numpy as jnp
from jax import lax
from jax.sharding import PartitionSpec as P

HIGH = lax.Precision.HIGHEST


def kernel(left, right):
    cross = jnp.dot(left, right.T, preferred_element_type=jnp.float32)
    left_sq = jnp.sum(jnp.square(left.astype(jnp.float32)), axis=1)
    right_sq = jnp.sum(jnp.square(right.astype(jnp.float32)), axis=1)
    dist_sq = left_sq[:, None] + right_sq[None, :] - 2.0 * cross
    return jnp.exp(-jnp.sqrt(jnp.maximum(dist_sq, 0.0)))


def correction(rows, subset_points, lift):
    return jnp.dot(
        kernel(
            rows,
            lax.all_gather(subset_points.astype(jnp.float32), "center", axis=0, tiled=True).astype(
                jnp.bfloat16
            ),
        ),
        lax.all_gather(lift, "center", axis=0, tiled=True),
        precision=HIGH,
    )


def shards(centers, weights, batch_index, targets, subset_points, eigvecs, shrink):
    p_local = centers.shape[0]
    first = lax.axis_index("center") * p_local
    local_index = batch_index - first
    picker = (local_index[:, None] == jnp.arange(p_local, dtype=jnp.int32)[None, :]).astype(
        jnp.bfloat16
    )
    chosen = jnp.dot(picker, centers, preferred_element_type=jnp.float32)
    batch = lax.psum(chosen, "center").astype(jnp.bfloat16)
    batch_kernel = kernel(batch, centers)
    pred = lax.psum(jnp.dot(batch_kernel, weights, precision=HIGH), "center")
    resid = pred - targets
    subset_kernel = kernel(subset_points, batch)
    proj_part = jnp.dot(eigvecs.T, jnp.dot(subset_kernel, resid, precision=HIGH), precision=HIGH)
    proj = lax.psum(proj_part, ("dp", "center"))
    lift = jnp.dot(eigvecs, shrink[:, None] * proj, precision=HIGH)
    grad_part = jnp.dot(batch_kernel.T, resid, precision=HIGH)
    scale = jnp.sqrt(jnp.float32(batch_index.shape[0] * lax.axis_size("dp")))
    grad = lax.psum(grad_part, "dp")
    corr = correction(centers, subset_points, lift)
    return (grad - corr) / scale


def solution(mesh):
    return jax.shard_map(
        shards,
        mesh=mesh,
        in_specs=(
            P("center", None),
            P("center", None),
            P("dp"),
            P("dp", None),
            P("center", None),
            P("center", None),
            P(),
        ),
        out_specs=P("center", None),
        check_vma=False,
    )
```

profile of v0, /device:TPU:1, one launch (start us, length us, event | category | flops | bytes accessed | tf_op | source)
XLA Modules:
  0.0 1604.1 jit_solution(8550933777695353325)
XLA Ops:
  6.5 2.7 multiply_reduce_fusion.1
  9.3 3.0 fusion.23
  12.3 313.2 %all-reduce.10 = bf16[256,768]{1,0:T(8,128)(2,1)S(1)} all-reduce(f32[256,768]{1,0:T(8,128)S(1)} %fusion.23), channel_id=1, replica_groups=mesh['dp'=4,'center'=64] {'center'}, use_global_device_ids=true, to_apply=%region_0.0 | all-reduce | flops 196608 | bytes 1179648 | tf_op jit(solution)/shard_map/psum | solution.py:38
  325.5 0.2 multiply_reduce_fusion.2
  325.6 3.4 fusion.16
  329.0 0.0 copy-start.1
  329.0 1.3 copy-done.1
  330.3 2.6 fusion.43
  332.9 0.0 all-reduce.5.cloned.1.call-update
  333.0 0.0 all-reduce.9.cloned.1.call-start
  333.0 0.1 multiply_reduce_fusion.3
  333.1 0.3 fusion.31
  333.4 656.5 %all-reduce.5.cloned.1.call-done = f32[256,256]{1,0:T(8,128)} async-done(((f32[256,256]{1,0:T(8,128)}), f32[256,256]{1,0:T(8,128)}) %all-reduce.5.cloned.1.call-update) | async-done | bytes 262160 | tf_op jit(solution)/shard_map/psum | solution.py:40
  989.9 1.2 fusion.34
  991.1 1.1 convolution_bitcast_fusion
  992.2 0.0 all-reduce.9.cloned.1.call-update
  992.2 0.0 all-gather.3.cloned.1.call-start
  992.3 0.7 all-gather.3.cloned.1.call-update
  992.9 0.0 all-reduce.7.cloned.1.call-start
  993.0 6.4 fusion.36
  999.4 0.0 all-reduce.7.cloned.1.call-update
  999.4 0.2 all-gather.5.cloned.1.call-start
  999.7 265.8 %all-reduce.9.cloned.1.call-done = f32[200,256]{1,0:T(8,128)} async-done(((f32[200,256]{1,0:T(8,128)}), f32[200,256]{1,0:T(8,128)}) %all-reduce.9.cloned.1.call-update) | async-done | bytes 204816 | tf_op jit(solution)/shard_map/psum | solution.py:44
  1265.4 1.8 convolution_bitcast_fusion.1
  1267.3 0.0 all-gather.5.cloned.1.call-update
  1267.3 120.7 %all-gather.3.cloned.1.call-done = bf16[2048,768]{1,0:T(8,128)(2,1)} async-done(((bf16[32,768]{1,0:T(8,128)(2,1)}), bf16[2048,768]{1,0:T(8,128)(2,1)}) %all-gather.3.cloned.1.call-update) | async-done | bytes 3145744 | tf_op jit(solution)/shard_map/all_gather | solution.py:21
  1387.9 2.7 multiply_reduce_fusion
  1390.7 0.1 copy-done.2
  1390.8 11.4 fusion.44
  1402.2 51.5 %all-reduce.7.cloned.1.call-done = f32[2048,256]{1,0:T(8,128)} async-done(((f32[2048,256]{1,0:T(8,128)}), f32[2048,256]{1,0:T(8,128)}) %all-reduce.7.cloned.1.call-update) | async-done | bytes 2097168 | tf_op jit(solution)/shard_map/psum | solution.py:48
  1453.7 119.5 %all-gather.5.cloned.1.call-done = f32[2048,256]{1,0:T(8,128)} async-done(((f32[32,256]{1,0:T(8,128)}), f32[2048,256]{1,0:T(8,128)}) %all-gather.5.cloned.1.call-update) | async-done | bytes 2097168 | tf_op jit(solution)/shard_map/all_gather | solution.py:25
  1573.2 24.4 %fusion.20 = f32[2048,256]{1,0:T(8,128)} fusion(f32[2048,256]{1,0:T(8,128)} %all-reduce.7.cloned.1.call-done, f32[2048,256]{1,0:T(8,128)} %all-gather.5.cloned.1.call-done, f32[2048,2048]{1,0:T(8,128)} %fusion.44, f32[2048]{0:T(1024)S(1)} %multiply_reduce_fusion, f32[2048]{0:T(1024)S(1)} %multiply_reduce_fusion.1), kind=kOutput, calls=%fused_computation.21 | convolution fusion | flops 12906921984 | bytes 23085056 | tf_op jit(solution)/shard_map/dot_general | solution.py:18
  (15 shorter events, 0.0 us)
Async XLA Ops:
  6.5 323.8 %copy-start = (f32[2048,256]{1,0:T(8,128)S(1)}, f32[2048,256]{1,0:T(8,128)}, u32[]{:S(2)}) copy-start(f32[2048,256]{1,0:T(8,128)} %param.8) | copy-start | bytes 6291460
  6.5 2.7 copy-start.7
  6.5 983.4 %all-reduce.5.cloned.1.call-start = ((), (), s32[]{:S(2)}) async-start(), calls=%async_computation | async-start | bytes 524288 | tf_op jit(solution)/shard_map/psum | solution.py:40
  329.0 1.3 copy-start.1
  330.3 2.7 copy-start.4
  330.3 659.6 %copy-start.3 = (f32[256,256]{1,0:T(8,128)S(1)}, f32[256,256]{1,0:T(8,128)}, u32[]{:S(2)}) copy-start(f32[256,256]{1,0:T(8,128)} %param.10) | copy-start | bytes 786436
  330.3 660.8 %copy-start.5 = (f32[32,200]{1,0:T(8,128)S(1)}, f32[32,200]{1,0:T(8,128)}, u32[]{:S(2)}) copy-start(f32[32,200]{1,0:T(8,128)} %param.12) | copy-start | bytes 76804
  333.0 932.5 %all-reduce.9.cloned.1.call-start = ((), (), s32[]{:S(2)}) async-start(), calls=%async_computation.3 | async-start | bytes 409600 | tf_op jit(solution)/shard_map/psum | solution.py:44
  992.2 395.7 %all-gather.3.cloned.1.call-start = ((), (), s32[]{:S(2)}) async-start(), calls=%async_computation.2 | async-start | bytes 3194880 | tf_op jit(solution)/shard_map/all_gather | solution.py:21
  992.9 460.7 %all-reduce.7.cloned.1.call-start = ((), (), s32[]{:S(2)}) async-start(), calls=%async_computation.1 | async-start | bytes 4194304 | tf_op jit(solution)/shard_map/psum | solution.py:48
  999.4 266.0 %copy-start.6 = (f32[200]{0:T(256)S(1)}, f32[200]{0:T(256)}, u32[]{:S(2)}) copy-start(f32[200]{0:T(256)} %param.13) | copy-start | bytes 2404
  999.4 573.8 %all-gather.5.cloned.1.call-start = ((), (), s32[]{:S(2)}) async-start(), calls=%async_computation.4 | async-start | bytes 2129920 | tf_op jit(solution)/shard_map/all_gather | solution.py:25
  1387.9 2.8 copy-start.2
Sparse Core Ops, SparseCore 0:
  333.1 656.7 all-reduce.4
  996.3 269.0 all-reduce.8
  1269.7 118.1 all-gather.2
  1390.7 62.9 all-reduce.6
  1457.1 116.0 all-gather.4
where the time goes:
time: 1610 us; the launch traced here: 1600 us
  waiting for transfers between devices  1210 us (75%)
  blocking collectives  313 us (19%)
  matrix products  55.5 us (3%)
    psum x1, waiting for transfers between devices, shards(): pred = lax.psum(jnp.dot(batch_kernel, weights, precision=HIGH), 'center')  656 us
    psum x1, blocking collectives, shards(): batch = lax.psum(chosen, 'center').astype(jnp.bfloat16)  313 us
    psum x1, waiting for transfers between devices, shards(): proj = lax.psum(proj_part, ('dp', 'center'))  266 us
    all_gather x1, waiting for transfers between devices, correction(): lax.all_gather(subset_points.astype(jnp.float32), 'center', axis=0, tiled...  121 us
    all_gather x1, waiting for transfers between devices, correction(): lax.all_gather(lift, 'center', axis=0, tiled=True)  119 us
    psum x1, waiting for transfers between devices, shards(): grad = lax.psum(grad_part, 'dp')  51.5 us
  transfers between devices with their start and end apart: 5, of which 5 were waited for; matrix products, arithmetic and copies ran while one was open for 1% of the time, Pallas kernels for 0%

commit v1 on v0

v1 whole, which is shorter than its diff:
```python
import jax
import jax.numpy as jnp
from jax import lax
from jax.experimental import pallas as pl
from jax.experimental.pallas import tpu as pltpu
from jax.sharding import PartitionSpec as P

MESH = pl.DeviceIdType.MESH
NY, NXH, NZ = 4, 2, 8
NX = 4
NYZ = NY * NZ
D, HALF, OUTS, Q, QP = 768, 384, 256, 200, 256
ROWS, BD, BATCH, SUBSET = 2048, 256, 1024, 2048
BF, F32 = jnp.bfloat16, jnp.float32
NT = (((1,), (1,)), ((), ()))
NN = (((1,), (0,)), ((), ()))


def dot(a, b, dims=NN):
    return lax.dot_general(a, b, dims, preferred_element_type=F32)


def split(x):
    hi = x.astype(BF)
    return hi, (x - hi.astype(F32)).astype(BF)


def dot3(ah, al, bh, bl, dims=NN):
    return dot(ah, bh, dims) + dot(ah, bl, dims) + dot(al, bh, dims)


def laplace(left_sq, right_sq, cross):
    dist_sq = jnp.maximum(left_sq + right_sq - 2.0 * cross, 1e-30)
    return jnp.exp(-(dist_sq * lax.rsqrt(dist_sq)))


def col_sq(x):
    sq = jnp.sum(jnp.square(x.astype(F32)), axis=1, keepdims=True)
    return jnp.broadcast_to(sq, (x.shape[0], 128))


def row_sq(x):
    hi, lo = split(jnp.square(x.astype(F32)))
    ones = jnp.ones((8, x.shape[1]), BF)
    return dot(ones, hi, NT) + dot(ones, lo, NT)


def widen(col, n):
    return jnp.concatenate([col] * (n // 128), axis=1)


def body(
    idx_ref, shr_ref, c_hbm, w_hbm, t_hbm, s_hbm, e_hbm, out_hbm,
    c_v, w_v, t_v, e_v, e_pad, out_v,
    chosen, rsb, xsb, xrb, ball, sbuf, ebuf,
    wt, tt, c_col, b_col, b_row, s_row, kcb,
    pred, rsp, xsp, xrp, rall, rhl, gbuf, mbuf, hbuf,
    lsem, osem, ss_yz, rs_yz, ss_m, rs_m,
):
    dp, ce = lax.axis_index("dp"), lax.axis_index("center")
    xlo, core = lax.div(dp, 2), lax.rem(dp, 2)
    y, xhi, z = lax.div(ce, 16), lax.rem(lax.div(ce, 8), 2), lax.rem(ce, 8)
    x = xhi * 2 + xlo
    chunk = y * NZ + z
    first = ce * ROWS

    def yz_peer(k):
        py = lax.rem(y + lax.div(k, NZ), NY)
        pz = lax.rem(z + lax.rem(k, NZ), NZ)
        return (dp, (py * NXH + xhi) * NZ + pz), py * NZ + pz

    def z_peer(j):
        return (dp, (y * NXH + xhi) * NZ + lax.rem(z + j, NZ))

    def y_peer(j):
        return (dp, (lax.rem(y + j, NY) * NXH + xhi) * NZ + z)

    def x_peer(j):
        px = lax.rem(x + j, NX)
        return (lax.rem(px, 2) * 2 + core, (y * NXH + lax.div(px, 2)) * NZ + z)

    sib = (xlo * 2 + 1 - core, ce)
    dpx = (1 - xlo) * 2 + core

    used = []

    def remote(src, dst, peer):
        slot = len(used)
        used.append(None)
        cp = pltpu.make_async_remote_copy(
            src_ref=src, dst_ref=dst, send_sem=ss_m.at[slot], recv_sem=rs_m.at[slot],
            device_id=peer, device_id_type=MESH,
        )
        cp.start()
        used[slot] = cp
        return cp

    def yz_copy(phase, k, src, dst, peer):
        return pltpu.make_async_remote_copy(
            src_ref=src, dst_ref=dst, send_sem=ss_yz.at[phase, k - 1],
            recv_sem=rs_yz.at[phase, k - 1], device_id=peer, device_id_type=MESH,
        )

    def recv(copies):
        for cp in copies:
            cp.wait_recv()

    def local(i, src, dst):
        cp = pltpu.make_async_copy(src, dst, lsem.at[i])
        cp.start()
        return cp

    ld_c = local(0, c_hbm, c_v)
    ld_e = local(1, e_hbm, e_v)
    ld_s = local(
        2,
        s_hbm.at[pl.ds(pl.multiple_of(xlo * 16, 16), 16), pl.ds(pl.multiple_of(core * HALF, 128), HALF)],
        sbuf.at[core, y, x, z],
    )
    ld_t = local(3, t_hbm, t_v)
    ld_w = local(4, w_hbm, w_v)

    barrier = pltpu.get_barrier_semaphore()

    def greet(k, carry):
        pl.semaphore_signal(barrier, inc=1, device_id=yz_peer(k)[0], device_id_type=MESH)
        return carry

    lax.fori_loop(1, NYZ, greet, 0)
    for j in range(1, NX):
        pl.semaphore_signal(barrier, inc=1, device_id=x_peer(j), device_id_type=MESH)
    pl.semaphore_signal(barrier, inc=1, device_id=sib, device_id_type=MESH)

    e_pad[...] = jnp.zeros_like(e_pad)
    ld_e.wait()
    e_pad[:, :Q] = e_v[...]
    e_hi, e_lo = split(e_pad[pl.ds(pl.multiple_of(xlo * 16, 16), 16), :])
    ebuf[core, x, y, z] = jnp.where(core == 0, e_hi.astype(F32), e_lo.astype(F32)).astype(BF)
    idx_col = jnp.transpose(jnp.broadcast_to((idx_ref[...] - first).astype(F32), (128, BD)))
    ld_c.wait()
    chosen_f = jnp.zeros((BD, D), F32)
    for b in range(ROWS // 256):
        iota = lax.broadcasted_iota(jnp.int32, (BD, 256), 1).astype(F32) + float(b * 256)
        pick = jnp.where(widen(idx_col, 256) == iota, 1.0, 0.0).astype(BF)
        chosen_f += dot(pick, c_v[b * 256:(b + 1) * 256, :])
    chosen_b = chosen_f.astype(BF)
    chosen[0:16] = chosen_b[:, :HALF].reshape(16, 16, HALF)
    chosen[16:32] = chosen_b[:, HALF:].reshape(16, 16, HALF)
    ld_s.wait()
    pl.semaphore_wait(barrier, NYZ - 1 + NX)

    def send_b(k, carry):
        peer, pc = yz_peer(k)
        yz_copy(0, k, chosen.at[pc], rsb.at[k - 1], peer).start()
        return carry

    lax.fori_loop(1, NYZ, send_b, 0)

    s_z = [remote(sbuf.at[core, y, x, z], sbuf.at[core, y, x, z], z_peer(j)) for j in range(1, NZ)]
    e_z = [remote(ebuf.at[core, x, y, z], ebuf.at[core, x, y, z], z_peer(j)) for j in range(1, NZ)]

    ld_w.wait()

    def prep(b, carry):
        rows = pl.ds(pl.multiple_of(b * 256, 256), 256)
        hi, lo = split(jnp.transpose(w_v[rows, :]))
        wt[0, b] = hi
        wt[1, b] = lo
        c_col[rows, :] = col_sq(c_v[rows, :])
        return carry

    lax.fori_loop(0, ROWS // 256, prep, 0)
    ld_t.wait()
    tt[...] = jnp.transpose(t_v[...]).reshape(NYZ, 8, BD)

    def add_b(k, acc):
        yz_copy(0, k, chosen.at[0], rsb.at[k - 1], sib).wait_recv()
        return acc + rsb[k - 1].astype(F32)

    part_b = lax.fori_loop(1, NYZ, add_b, chosen[chunk].astype(F32))
    xsb[...] = part_b.astype(BF)
    b_x = remote(xsb, xrb, x_peer(2))
    recv(s_z)
    s_x = [remote(sbuf.at[core, y, x], sbuf.at[core, y, x], x_peer(j)) for j in range(1, NX)]
    recv(e_z)
    e_y = [remote(ebuf.at[core, x, y], ebuf.at[core, x, y], y_peer(j)) for j in range(1, NY)]
    recv([b_x])
    ball[dp, chunk] = (part_b + xrb[...].astype(F32)).astype(BF)

    def send_b2(k, carry):
        peer, pc = yz_peer(k)
        yz_copy(1, k, ball.at[dp, chunk], ball.at[dp, chunk], peer).start()
        return carry

    lax.fori_loop(1, NYZ, send_b2, 0)
    recv(s_x)
    s_y = [remote(sbuf.at[core, y], sbuf.at[core, y], y_peer(j)) for j in range(1, NY)]
    recv(e_y)
    e_x = [remote(ebuf.at[core, x], ebuf.at[core, x], x_peer(j)) for j in range(1, NX)]

    def got_b2(k, carry):
        yz_copy(1, k, ball.at[dp, chunk], ball.at[dp, chunk], sib).wait_recv()
        return carry

    lax.fori_loop(1, NYZ, got_b2, 0)
    b_r = remote(ball.at[dp, pl.ds(0, 16)], ball.at[dp, pl.ds(0, 16)], x_peer(1))
    b_l = remote(ball.at[dp, pl.ds(16, 16)], ball.at[dp, pl.ds(16, 16)], x_peer(3))
    b_s = [remote(ball.at[dp], ball.at[dp], sib)]

    def b_halves(d):
        return ball[d, 0:16].reshape(BD, HALF), ball[d, 16:32].reshape(BD, HALF)

    def norms_b(d):
        b0, b1 = b_halves(d)
        b_row[d] = row_sq(b0) + row_sq(b1)
        b_col[d] = col_sq(b0) + col_sq(b1)

    def k_rows(d, b, b0, b1):
        rows = pl.ds(pl.multiple_of(b * 256, 256), 256)
        cross = dot(c_v[rows, :HALF], b0, NT) + dot(c_v[rows, HALF:], b1, NT)
        kern = laplace(widen(c_col[rows, :], BD), b_row[d][0:1, :], cross)
        kcb[d, rows, :] = kern
        return kern

    def k_block(d):
        norms_b(d)
        b0, b1 = b_halves(d)

        def step(b, carry):
            k_rows(d, b, b0, b1)
            return carry

        lax.fori_loop(0, ROWS // 256, step, 0)

    norms_b(dp)
    own0, own1 = b_halves(dp)

    pred[...] = jnp.zeros_like(pred)

    def pred_step(b, carry):
        kh, kl = split(k_rows(dp, b, own0, own1))
        pred[...] += dot3(wt[0, b], wt[1, b], kh, kl).reshape(NYZ, 8, BD)
        return carry

    lax.fori_loop(0, ROWS // 256, pred_step, 0)

    def send_p(k, carry):
        peer, pc = yz_peer(k)
        yz_copy(2, k, pred.at[pc], rsp.at[k - 1], peer).start()
        return carry

    lax.fori_loop(1, NYZ, send_p, 0)
    recv([b_r, b_l])
    b_s += [remote(ball.at[dpx], ball.at[dpx], sib)]
    k_block(dpx)

    def add_p(k, acc):
        yz_copy(2, k, pred.at[0], rsp.at[k - 1], sib).wait_recv()
        return acc + rsp[k - 1]

    part_p = lax.fori_loop(1, NYZ, add_p, pred[chunk])
    xsp[...] = part_p
    p_x = remote(xsp, xrp, x_peer(2))
    recv(e_x)
    e_s = [remote(ebuf.at[core], ebuf.at[core], sib)]
    recv([p_x])
    rall[dp, chunk] = part_p + xrp[...] - tt[chunk]
    r_z = [remote(rall.at[dp, chunk], rall.at[dp, chunk], z_peer(j)) for j in range(1, NZ)]
    recv(b_s)
    k_block(xlo * 2 + 1 - core)
    line = pl.ds(pl.multiple_of(y * NZ, NZ), NZ)
    recv(r_z)
    r_y = [remote(rall.at[dp, line], rall.at[dp, line], y_peer(j)) for j in range(1, NY)]
    recv(s_y)
    s_s = [remote(sbuf.at[core], sbuf.at[core], sib)]
    k_block((1 - xlo) * 2 + 1 - core)
    recv(r_y)
    r_r = remote(rall.at[dp, pl.ds(0, 16)], rall.at[dp, pl.ds(0, 16)], x_peer(1))
    r_l = remote(rall.at[dp, pl.ds(16, 16)], rall.at[dp, pl.ds(16, 16)], x_peer(3))
    r_s = [remote(rall.at[dp], rall.at[dp], sib)]
    recv(e_s + s_s)

    for yy in range(NY):
        s_row[yy] = row_sq(sbuf[0, yy].reshape(512, HALF)) + row_sq(sbuf[1, yy].reshape(512, HALF))

    def subset_product(x0, x1, left):
        acc = jnp.zeros((512, QP), F32)
        for yy in range(NY):
            cross = dot(x0, sbuf[0, yy].reshape(512, HALF), NT) + dot(x1, sbuf[1, yy].reshape(512, HALF), NT)
            kh, kl = split(laplace(widen(left, 512), s_row[yy][0:1, :], cross))
            acc += dot3(kh, kl, ebuf[0, :, yy].reshape(512, QP), ebuf[1, :, yy].reshape(512, QP))
        return acc

    def g_step(b, carry):
        rows = pl.ds(pl.multiple_of(core * 1024 + b * 512, 512), 512)
        g = subset_product(c_v[rows, :HALF], c_v[rows, HALF:], c_col[rows, :]) * shr_ref[...]
        hi, lo = split(g)
        gbuf[0, rows, :] = hi
        gbuf[1, rows, :] = lo
        return carry

    lax.fori_loop(0, 2, g_step, 0)
    g_rows = pl.ds(pl.multiple_of(core * 1024, 1024), 1024)
    gm_s = [remote(gbuf.at[:, g_rows], gbuf.at[:, g_rows], sib)]
    m_rows = pl.ds(pl.multiple_of(core * 512, 512), 512)
    two = pl.ds(core * 2, 2)
    m_hi, m_lo = split(subset_product(
        ball[two, 0:16].reshape(512, HALF), ball[two, 16:32].reshape(512, HALF), b_col[two].reshape(512, 128)
    ))
    mbuf[0, m_rows, :] = m_hi
    mbuf[1, m_rows, :] = m_lo
    gm_s += [remote(mbuf.at[:, m_rows], mbuf.at[:, m_rows], sib)]
    recv([r_r, r_l])
    r_s += [remote(rall.at[dpx], rall.at[dpx], sib)]
    recv(gm_s)

    def h_step(b, carry):
        rows = pl.ds(pl.multiple_of(b * 256, 256), 256)
        gh, gl = gbuf[0, rows, :], gbuf[1, rows, :]
        for d in range(4):
            m = slice(d * 256, (d + 1) * 256)
            hi, lo = split(kcb[d, rows, :] - dot3(gh, gl, mbuf[0, m, :], mbuf[1, m, :], NT))
            hbuf[0, d, rows, :] = hi
            hbuf[1, d, rows, :] = lo
        return carry

    lax.fori_loop(0, ROWS // 256, h_step, 0)

    recv(r_s)
    for d in range(4):
        hi, lo = split(rall[d].reshape(OUTS, BD) * (1.0 / BATCH**0.5))
        rhl[0, d] = hi
        rhl[1, d] = lo

    def out_copy(b):
        rows = pl.ds(pl.multiple_of(b * 256, 256), 256)
        return pltpu.make_async_copy(out_v.at[rows, :], out_hbm.at[rows, :], osem.at[b])

    def out_step(b, carry):
        rows = pl.ds(pl.multiple_of(b * 256, 256), 256)
        acc = jnp.zeros((256, OUTS), F32)
        for d in range(4):
            acc += dot3(hbuf[0, d, rows, :], hbuf[1, d, rows, :], rhl[0, d], rhl[1, d], NT)
        out_v[rows, :] = acc
        out_copy(b).start()
        return carry

    lax.fori_loop(0, ROWS // 256, out_step, 0)

    def out_wait(b, carry):
        out_copy(b).wait()
        return carry

    lax.fori_loop(0, ROWS // 256, out_wait, 0)

    for cp in used:
        cp.wait_send()

    def sent(k, carry):
        yz_copy(0, k, chosen.at[0], rsb.at[0], sib).wait_send()
        yz_copy(1, k, ball.at[0, 0], ball.at[0, 0], sib).wait_send()
        yz_copy(2, k, pred.at[0], rsp.at[0], sib).wait_send()
        return carry

    lax.fori_loop(1, NYZ, sent, 0)


N_MISC = 64


def shards(centers, weights, batch_index, targets, subset_points, eigvecs, shrink):
    shr = jnp.pad(shrink, (0, QP - Q)).reshape(1, QP)
    v = pltpu.VMEM
    any_spec = pl.BlockSpec(memory_space=pl.ANY)
    vm = pl.BlockSpec(memory_space=pltpu.VMEM)
    return pl.pallas_call(
        body,
        out_shape=jax.ShapeDtypeStruct((ROWS, OUTS), F32),
        in_specs=[vm, vm] + [any_spec] * 5,
        out_specs=any_spec,
        scratch_shapes=[
            v((ROWS, D), BF), v((ROWS, OUTS), F32), v((BD, OUTS), F32), v((32, Q), F32), v((32, QP), F32), v((ROWS, OUTS), F32),
            v((NYZ, 16, HALF), BF), v((NYZ - 1, 16, HALF), BF), v((16, HALF), BF), v((16, HALF), BF), v((4, NYZ, 16, HALF), BF),
            v((2, NY, NX, NZ, 16, HALF), BF), v((2, NX, NY, NZ, 16, QP), BF),
            v((2, ROWS // 256, OUTS, 256), BF), v((NYZ, 8, BD), F32), v((ROWS, 128), F32), v((4, BD, 128), F32), v((4, 8, BD), F32), v((NY, 8, 512), F32), v((4, ROWS, BD), F32),
            v((NYZ, 8, BD), F32), v((NYZ - 1, 8, BD), F32), v((8, BD), F32), v((8, BD), F32), v((4, NYZ, 8, BD), F32), v((2, 4, OUTS, BD), BF),
            v((2, ROWS, QP), BF), v((2, BATCH, QP), BF), v((2, 4, ROWS, BD), BF),
            pltpu.SemaphoreType.DMA((5,)), pltpu.SemaphoreType.DMA((ROWS // 256,)),
            pltpu.SemaphoreType.DMA((3, NYZ - 1)), pltpu.SemaphoreType.DMA((3, NYZ - 1)),
            pltpu.SemaphoreType.DMA((N_MISC,)), pltpu.SemaphoreType.DMA((N_MISC,)),
        ],
        compiler_params=pltpu.CompilerParams(collective_id=0, has_side_effects=True, vmem_limit_bytes=60 * 2**20),
        name="eigenpro_step",
    )(batch_index.reshape(1, BD), shr, centers, weights, targets, subset_points, eigvecs)


def solution(mesh):
    return jax.shard_map(
        shards,
        mesh=mesh,
        in_specs=(
            P("center", None),
            P("center", None),
            P("dp"),
            P("dp", None),
            P("center", None),
            P("center", None),
            P(),
        ),
        out_specs=P("center", None),
        check_vma=False,
    )
```

time: 1610 us -> 110 us (0.07)
  waiting for transfers between devices: 1210 us -> 0 us
  blocking collectives: 313 us -> 0 us
  Pallas kernels: 0 us -> 106 us
  matrix products: 55.5 us -> 0 us
    psum x3 -> x0, waiting for transfers between devices: 974 us -> none  [the longest x1 656 us: shards(): pred = lax.psum(jnp.dot(batch_kernel, weights, precision=HIGH), 'center')]
    psum x1 -> x0, blocking collectives: 313 us -> none  [shards(): batch = lax.psum(chosen, 'center').astype(jnp.bfloat16)]
    all_gather x2 -> x0, waiting for transfers between devices: 240 us -> none  [the longest x1 121 us: correction(): lax.all_gather(subset_points.astype(jnp.float32), 'center', axis=0, tiled...]
    pallas_call x0 -> x1, Pallas kernels: none -> 106 us  [shards(): pl.pallas_call(body, out_shape=jax.ShapeDtypeStruct((ROWS, OUTS), F32), i...]
    dot_general x10 -> x0, matrix products: 55.5 us -> none  [the longest x1 24.4 us: correction(): jnp.dot(kernel(rows, lax.all_gather(subset_points.astype(jnp.float32), 'c...]
  transfers between devices with their start and end apart: 5 -> 0, of which waited for: 5 -> 0; matrix products, arithmetic and copies ran while one was open for 1% -> 0% of each run, Pallas kernels for 0% -> 0%
where the time goes in v1:
time: 110 us
  Pallas kernels  106 us (96%)
  local copies, waits for them, and re-layouts  4.29 us (4%)
    pallas_call x1, Pallas kernels, shards(): pl.pallas_call(body, out_shape=jax.ShapeDtypeStruct((ROWS, OUTS), F32), i...  106 us
    unnamed x1, local copies, waits for them, and re-layouts  3.05 us

profile of v1, /device:TPU:1, one launch (start us, length us, event | category | flops | bytes accessed | tf_op | source)
XLA Modules:
  0.0 109.8 jit_solution(15680539112406060743)
XLA Ops:
  0.0 1.2 %pad.4 = f32[256]{0:T(256)} pad(f32[200]{0:T(256)} %param.13, f32[]{:T(128)} %constant.2.clone.1), padding=0_56 | pad | bytes 1828 | tf_op jit(solution)/shard_map/jit(_pad)/pad | solution.py:372
  1.2 105.5 %eigenpro_step.1 = f32[2048,256]{1,0:T(8,128)} custom-call(s32[1,256]{1,0:T(1,128)} %bitcast.3, f32[1,256]{1,0:T(1,128)} %bitcast.2, bf16[2048,768]{1,0:T(8,128)(2,1)} %c_hbm.1, f32[2048,256]{1,0:T(8,128)} %w_hbm.1, f32[256,256]{1,0:T(8,128)} %t_hbm.1, bf16[32,768]{1,0:T(8,128)(2,1)} %s_hbm.1, f32[32,200]{1,0:T(8,128)} %e_hbm.1), custom_call_target="tpu_custom_call" | custom-call | tf_op jit(solution)/shard_map/eigenpro_step/pallas_call | solution.py:376
  106.8 3.0 %copy.9 = f32[2048,256]{1,0:T(8,128)} copy(f32[2048,256]{1,0:T(8,128)} %eigenpro_step.1) | data formatting | bytes 4194304

commit v2 on v1

v2 whole, which is shorter than its diff:
```python
import jax
import jax.numpy as jnp
from jax import lax
from jax.experimental import pallas as pl
from jax.experimental.pallas import tpu as pltpu
from jax.sharding import PartitionSpec as P

MESH = pl.DeviceIdType.MESH
NY, NXH, NZ = 4, 2, 8
NX = 4
NYZ = NY * NZ
D, HALF, OUTS, Q, QP = 768, 384, 256, 200, 256
ROWS, BD, BATCH, SUBSET = 2048, 256, 1024, 2048
BF, F32 = jnp.bfloat16, jnp.float32
FAR_Z = (4, 3, 5, 2, 6, 1, 7)
NT = (((1,), (1,)), ((), ()))
NN = (((1,), (0,)), ((), ()))


def dot(a, b, dims=NN):
    return lax.dot_general(a, b, dims, preferred_element_type=F32)


def split(x):
    hi = x.astype(BF)
    return hi, (x - hi.astype(F32)).astype(BF)


def dot3(ah, al, bh, bl, dims=NN):
    return dot(ah, bh, dims) + dot(ah, bl, dims) + dot(al, bh, dims)


def laplace(left_sq, right_sq, cross):
    dist_sq = jnp.maximum(left_sq + right_sq - 2.0 * cross, 1e-30)
    return jnp.exp(-(dist_sq * lax.rsqrt(dist_sq)))


def col_sq(x):
    sq = jnp.sum(jnp.square(x.astype(F32)), axis=1, keepdims=True)
    return jnp.broadcast_to(sq, (x.shape[0], 128))


def row_sq(x):
    hi, lo = split(jnp.square(x.astype(F32)))
    ones = jnp.ones((8, x.shape[1]), BF)
    return dot(ones, hi, NT) + dot(ones, lo, NT)


def widen(col, n):
    return jnp.concatenate([col] * (n // 128), axis=1)


def body(
    idx_ref, shr_ref, c_hbm, w_hbm, t_hbm, s_hbm, e_hbm, out_ref,
    c_v, w_v, t_v, e_v, e_pad, shr_pad,
    chosen, rsby, zsrc, rsbz, xsb, xrb, ball, sbuf, ebuf,
    wt, tt, c_col, b_row, s_row, kb,
    pred, rsp, xsp, xrp, rall, rhl, gbuf, mbuf, lacc,
    lsem, ss_yz, rs_yz, ss_m, rs_m,
):
    dp, ce = lax.axis_index("dp"), lax.axis_index("center")
    xlo, core = lax.div(dp, 2), lax.rem(dp, 2)
    y, xhi, z = lax.div(ce, 16), lax.rem(lax.div(ce, 8), 2), lax.rem(ce, 8)
    x = xhi * 2 + xlo
    chunk = y * NZ + z
    first = ce * ROWS

    def yz_peer(k):
        py = lax.rem(y + lax.div(k, NZ), NY)
        pz = lax.rem(z + lax.rem(k, NZ), NZ)
        return (dp, (py * NXH + xhi) * NZ + pz), py * NZ + pz

    def z_peer(j):
        return (dp, (y * NXH + xhi) * NZ + lax.rem(z + j, NZ))

    def y_peer(j):
        return (dp, (lax.rem(y + j, NY) * NXH + xhi) * NZ + z)

    def x_peer(j):
        px = lax.rem(x + j, NX)
        return (lax.rem(px, 2) * 2 + core, (y * NXH + lax.div(px, 2)) * NZ + z)

    sib = (xlo * 2 + 1 - core, ce)
    dpx = (1 - xlo) * 2 + core
    dps, dpxs = xlo * 2 + 1 - core, (1 - xlo) * 2 + 1 - core

    def slot(py, pz):
        return lax.rem(py, 2) * NZ + pz, slice(None), pl.ds(pl.multiple_of(lax.div(py, 2) * HALF, 128), HALF)

    lane = pl.ds(pl.multiple_of(core * HALF, 128), HALF)
    used, unsent = [], []

    def remote(src, dst, peer):
        slot = len(used)
        used.append(None)
        cp = pltpu.make_async_remote_copy(
            src_ref=src, dst_ref=dst, send_sem=ss_m.at[slot], recv_sem=rs_m.at[slot],
            device_id=peer, device_id_type=MESH,
        )
        cp.start()
        unsent.append(cp)
        return cp

    def drain():
        for cp in unsent:
            cp.wait_send()
        unsent.clear()

    def yz_copy(phase, k, src, dst, peer):
        return pltpu.make_async_remote_copy(
            src_ref=src, dst_ref=dst, send_sem=ss_yz.at[phase, k - 1],
            recv_sem=rs_yz.at[phase, k - 1], device_id=peer, device_id_type=MESH,
        )

    def recv(copies):
        for cp in copies:
            cp.wait_recv()

    def local(i, src, dst):
        cp = pltpu.make_async_copy(src, dst, lsem.at[i])
        cp.start()
        return cp

    ld_c = local(0, c_hbm, c_v)
    ld_e = local(1, e_hbm, e_v)
    ld_s = local(
        2,
        s_hbm.at[pl.ds(pl.multiple_of(xlo * 16, 16), 16), lane],
        sbuf.at[x, y, z, :, lane],
    )
    ld_t = local(3, t_hbm, t_v)
    ld_w = local(4, w_hbm, w_v)

    barrier = pltpu.get_barrier_semaphore()

    def greet(k, carry):
        pl.semaphore_signal(barrier, inc=1, device_id=yz_peer(k)[0], device_id_type=MESH)
        return carry

    lax.fori_loop(1, NYZ, greet, 0)
    for j in range(1, NX):
        pl.semaphore_signal(barrier, inc=1, device_id=x_peer(j), device_id_type=MESH)
    pl.semaphore_signal(barrier, inc=1, device_id=sib, device_id_type=MESH)

    e_pad[...] = jnp.zeros_like(e_pad)
    ld_e.wait()
    e_pad[:, :Q] = e_v[...]
    shr_pad[...] = jnp.zeros_like(shr_pad)
    shr_pad[0:1, :Q] = shr_ref[...]
    e_hi, e_lo = split(e_pad[pl.ds(pl.multiple_of(xlo * 16, 16), 16), :])
    ebuf[core, y, x, z] = jnp.where(core == 0, e_hi.astype(F32), e_lo.astype(F32)).astype(BF)
    idx_col = jnp.transpose(jnp.broadcast_to((idx_ref[...] - first).astype(F32), (128, BD)))
    ld_c.wait()
    chosen_f = jnp.zeros((BD, D), F32)
    for b in range(ROWS // 256):
        iota = lax.broadcasted_iota(jnp.int32, (BD, 256), 1).astype(F32) + float(b * 256)
        pick = jnp.where(widen(idx_col, 256) == iota, 1.0, 0.0).astype(BF)
        chosen_f += dot(pick, c_v[b * 256:(b + 1) * 256, :])
    chosen_b = chosen_f.astype(BF)
    chosen[...] = chosen_b.reshape(16, 16, D)
    ld_s.wait()
    pl.semaphore_wait(barrier, NYZ - 1 + NX)

    b_y = []
    for i, o in enumerate(FAR_Z + (0,)):
        pz = lax.rem(z + o, NZ)
        b_y.append([
            remote(chosen.at[slot(lax.rem(y + j, NY), pz)], rsby.at[i, j - 1], y_peer(j)) for j in range(1, NY)
        ])

    s_z = [remote(sbuf.at[x, y, z, :, lane], sbuf.at[x, y, z, :, lane], z_peer(o)) for o in FAR_Z]
    e_z = [remote(ebuf.at[core, y, x, z], ebuf.at[core, y, x, z], z_peer(o)) for o in FAR_Z]

    b_z = []
    for i, o in enumerate(FAR_Z + (0,)):
        recv(b_y[i])
        part_b = chosen[slot(y, lax.rem(z + o, NZ))].astype(F32)
        for j in range(NY - 1):
            part_b += rsby[i, j].astype(F32)
        if o:
            zsrc[i] = part_b.astype(BF)
            b_z.append(remote(zsrc.at[i], rsbz.at[i], z_peer(o)))
    recv(s_z)
    s_y = [remote(sbuf.at[x, y, :, :, lane], sbuf.at[x, y, :, :, lane], y_peer(j)) for j in range(1, NY)]
    recv(e_z)
    e_x = [remote(ebuf.at[core, y, x], ebuf.at[core, y, x], x_peer(j)) for j in range(1, NX)]
    for i in range(NZ - 1):
        recv([b_z[i]])
        part_b += rsbz[i].astype(F32)
    xsb[...] = part_b.astype(BF)
    b_x = remote(xsb, xrb, x_peer(2))
    ld_w.wait()

    def prep(b, carry):
        rows = pl.ds(pl.multiple_of(b * 256, 256), 256)
        hi, lo = split(jnp.transpose(w_v[rows, :]))
        wt[0, b] = hi
        wt[1, b] = lo
        c_col[rows, :] = col_sq(c_v[rows, :])
        return carry

    lax.fori_loop(0, ROWS // 256, prep, 0)
    ld_t.wait()
    tt[...] = jnp.transpose(t_v[...]).reshape(NYZ, 8, BD)

    recv([b_x])
    here = (dp,) + slot(y, z)
    ball[here] = (xsb[...].astype(F32) + xrb[...].astype(F32)).astype(BF)

    own = ball.at[here]
    g_z = {o: remote(own, own, z_peer(o)) for o in FAR_Z}
    g_y = [remote(own, own, y_peer(j)) for j in range(1, NY)]
    recv(s_y)
    s_x = [remote(sbuf.at[x, :, :, :, lane], sbuf.at[x, :, :, :, lane], x_peer(j)) for j in range(1, NX)]
    s_s = [remote(sbuf.at[x, :, :, :, lane], sbuf.at[x, :, :, :, lane], sib)]
    for o in FAR_Z[::-1]:
        recv([g_z[o]])
        came = ball.at[(dp,) + slot(y, lax.rem(z + NZ - o, NZ))]
        g_y += [remote(came, came, y_peer(j)) for j in range(1, NY)]
    recv(e_x)
    e_y = [remote(ebuf.at[core, y], ebuf.at[core, y], y_peer(j)) for j in range(1, NY)]
    e_s = [remote(ebuf.at[core, y], ebuf.at[core, y], sib)]
    recv(g_y)
    b_s = [remote(ball.at[dp], ball.at[dp], sib)]
    b_r = remote(ball.at[dp, pl.ds(0, 8)], ball.at[dp, pl.ds(0, 8)], x_peer(1))
    b_l = remote(ball.at[dp, pl.ds(8, 8)], ball.at[dp, pl.ds(8, 8)], x_peer(3))

    def norms_b(d):
        b_row[d] = row_sq(ball[d].reshape(BD, D))

    def k_rows(d, b, n):
        rows = pl.ds(pl.multiple_of(b * n, n), n)
        cross = dot(c_v[rows, :], ball[d].reshape(BD, D), NT)
        hi, lo = split(laplace(widen(c_col[rows, :], BD), b_row[d][0:1, :], cross))
        kb[0, d, rows, :] = hi
        kb[1, d, rows, :] = lo
        return hi, lo

    def k_block(d):
        norms_b(d)

        def step(b, carry):
            k_rows(d, b, 512)
            return carry

        lax.fori_loop(0, ROWS // 512, step, 0, unroll=True)

    norms_b(dp)
    pred[...] = jnp.zeros_like(pred)

    def pred_step(b, carry):
        kh, kl = k_rows(dp, b, 256)
        pred[...] += dot3(wt[0, b], wt[1, b], kh, kl).reshape(NYZ, 8, BD)
        return carry

    lax.fori_loop(0, ROWS // 256, pred_step, 0, unroll=True)

    def send_p(i, carry):
        k = NYZ - i
        peer, pc = yz_peer(k)
        yz_copy(0, k, pred.at[pc], rsp.at[k - 1], peer).start()
        return carry

    lax.fori_loop(1, NYZ, send_p, 0)
    recv(b_s)
    k_block(dps)
    drain()
    recv([b_r, b_l])
    b_s2 = remote(ball.at[dpx], ball.at[dpx], sib)
    k_block(dpx)
    recv(e_y)
    e_s += [remote(ebuf.at[core, lax.rem(y + j, NY)], ebuf.at[core, lax.rem(y + j, NY)], sib) for j in range(1, NY)]
    recv([b_s2])
    k_block(dpxs)

    def subset_product(rows_b, left):
        n = rows_b.shape[0]
        acc = jnp.zeros((n, QP), F32)
        for xx in range(NX):
            for p in range(NY // 2):
                two = slice(2 * p, 2 * p + 2)
                cross = dot(rows_b, sbuf[xx, two].reshape(256, D), NT)
                kh, kl = split(laplace(widen(left, 256), s_row[xx][0:1, 256 * p:256 * p + 256], cross))
                acc += dot3(kh, kl, ebuf[0, two, xx].reshape(256, QP), ebuf[1, two, xx].reshape(256, QP))
        return acc

    def g_step(b):
        rows = pl.ds(pl.multiple_of(core * 1024 + b * 512, 512), 512)
        g = subset_product(c_v[rows, :], c_col[rows, :]) * -shr_pad[0:1, :]
        hi, lo = split(g)
        gbuf[0, rows, :] = hi
        gbuf[1, rows, :] = lo

    def add_p(k, acc):
        yz_copy(0, k, pred.at[0], rsp.at[k - 1], sib).wait_recv()
        return acc + rsp[k - 1]

    part_p = lax.fori_loop(1, NYZ, add_p, pred[chunk])
    xsp[...] = part_p
    p_x = remote(xsp, xrp, x_peer(2))
    recv([p_x])
    rall[dp, chunk] = xsp[...] + xrp[...] - tt[chunk]

    def send_r(i, carry):
        k = NYZ - i
        peer, pc = yz_peer(k)
        yz_copy(1, k, rall.at[dp, chunk], rall.at[dp, chunk], peer).start()
        return carry

    lax.fori_loop(1, NYZ, send_r, 0)
    recv(s_x)
    s_s += [remote(sbuf.at[lax.rem(x + j, NX), :, :, :, lane], sbuf.at[lax.rem(x + j, NX), :, :, :, lane], sib) for j in range(1, NX)]
    recv(e_s + s_s)
    for xx in range(NX):
        s_row[xx] = row_sq(sbuf[xx].reshape(512, D))
    b_part = ball[core * 2 + lax.div(y, 2), pl.ds(lax.rem(y, 2) * 8, 8)].reshape(128, D)
    m_mine = pl.ds(pl.multiple_of(core * 512 + y * 128, 128), 128)
    m_hi, m_lo = split(subset_product(b_part, col_sq(b_part)))
    mbuf[0, m_mine, :] = m_hi
    mbuf[1, m_mine, :] = m_lo
    m_y = [remote(mbuf.at[:, m_mine], mbuf.at[:, m_mine], y_peer(j)) for j in range(1, NY)]
    g_step(0)

    def got_r(k, carry):
        yz_copy(1, k, rall.at[dp, chunk], rall.at[dp, chunk], sib).wait_recv()
        return carry

    r_x = {}
    for j in (0, 1, 3, 2):
        lax.fori_loop(max(1, j * NZ), (j + 1) * NZ, got_r, 0)
        line_y = lax.rem(y + NY - j, NY)
        line = rall.at[dp, pl.ds(pl.multiple_of(line_y * NZ, NZ), NZ)]
        r_x[j] = remote(line, line, x_peer(1 + 2 * lax.div(line_y, 2)))
    r_s = remote(rall.at[dp], rall.at[dp], sib)
    g_step(1)
    g_rows = pl.ds(pl.multiple_of(core * 1024, 1024), 1024)
    gm_s = [remote(gbuf.at[:, g_rows], gbuf.at[:, g_rows], sib)]
    r_s2 = []
    for j in (0, 1, 3, 2):
        recv([r_x[j]])
        line = rall.at[dpx, pl.ds(pl.multiple_of(lax.rem(y + NY - j, NY) * NZ, NZ), NZ)]
        r_s2.append(remote(line, line, sib))
    recv(m_y)
    m_rows = pl.ds(pl.multiple_of(core * 512, 512), 512)
    gm_s += [remote(mbuf.at[:, m_rows], mbuf.at[:, m_rows], sib)]

    def split_r(d):
        hi, lo = split(rall[d].reshape(OUTS, BD) * (1.0 / BATCH**0.5))
        rhl[0, d] = hi
        rhl[1, d] = lo

    def k_out(rows, d):
        return dot3(kb[0, d, rows, :], kb[1, d, rows, :], rhl[0, d], rhl[1, d], NT)

    def lift_t(d):
        rows = pl.ds(pl.multiple_of(d * BD, BD), BD)
        return dot3(rhl[0, d], rhl[1, d], mbuf[0, rows, :], mbuf[1, rows, :])

    recv([r_s])
    split_r(dp)
    split_r(dps)

    def out_near(b, carry):
        rows = pl.ds(pl.multiple_of(b * 256, 256), 256)
        out_ref[rows, :] = k_out(rows, dp) + k_out(rows, dps)
        return carry

    lax.fori_loop(0, ROWS // 256, out_near, 0, unroll=True)
    recv(r_s2)
    split_r(dpx)
    split_r(dpxs)
    recv(gm_s)
    lacc[...] = lift_t(0) + lift_t(1) + lift_t(2) + lift_t(3)
    l_hi, l_lo = split(lacc[...])

    def out_far(b, carry):
        rows = pl.ds(pl.multiple_of(b * 256, 256), 256)
        corr = dot3(gbuf[0, rows, :], gbuf[1, rows, :], l_hi, l_lo, NT)
        out_ref[rows, :] += k_out(rows, dpx) + k_out(rows, dpxs) + corr
        return carry

    lax.fori_loop(0, ROWS // 256, out_far, 0, unroll=True)
    drain()

    def sent(k, carry):
        yz_copy(0, k, pred.at[0], rsp.at[0], sib).wait_send()
        yz_copy(1, k, rall.at[0, 0], rall.at[0, 0], sib).wait_send()
        return carry

    lax.fori_loop(1, NYZ, sent, 0)


N_MISC = 144


def shards(centers, weights, batch_index, targets, subset_points, eigvecs, shrink):
    v = pltpu.VMEM
    any_spec = pl.BlockSpec(memory_space=pl.ANY)
    vm = pl.BlockSpec(memory_space=pltpu.VMEM)
    return pl.pallas_call(
        body,
        out_shape=pltpu.VMEM((ROWS, OUTS), F32),
        in_specs=[vm, vm] + [any_spec] * 5,
        out_specs=vm,
        scratch_shapes=[
            v((ROWS, D), BF), v((ROWS, OUTS), F32), v((BD, OUTS), F32), v((32, Q), F32), v((32, QP), F32), v((8, QP), F32),
            v((16, 16, D), BF), v((NZ, NY - 1, 16, HALF), BF), v((NZ - 1, 16, HALF), BF), v((NZ - 1, 16, HALF), BF), v((16, HALF), BF), v((16, HALF), BF), v((4, 16, 16, D), BF),
            v((NX, NY, NZ, 16, D), BF), v((2, NY, NX, NZ, 16, QP), BF),
            v((2, ROWS // 256, OUTS, 256), BF), v((NYZ, 8, BD), F32), v((ROWS, 128), F32), v((4, 8, BD), F32), v((NX, 8, 512), F32), v((2, 4, ROWS, BD), BF),
            v((NYZ, 8, BD), F32), v((NYZ - 1, 8, BD), F32), v((8, BD), F32), v((8, BD), F32), v((4, NYZ, 8, BD), F32), v((2, 4, OUTS, BD), BF),
            v((2, ROWS, QP), BF), v((2, BATCH, QP), BF), v((OUTS, QP), F32),
            pltpu.SemaphoreType.DMA((5,)),
            pltpu.SemaphoreType.DMA((2, NYZ - 1)), pltpu.SemaphoreType.DMA((2, NYZ - 1)),
            pltpu.SemaphoreType.DMA((N_MISC,)), pltpu.SemaphoreType.DMA((N_MISC,)),
        ],
        compiler_params=pltpu.CompilerParams(collective_id=0, has_side_effects=True, vmem_limit_bytes=56 * 2**20),
        name="eigenpro_step",
    )(batch_index.reshape(1, BD), shrink.reshape(1, Q), centers, weights, targets, subset_points, eigvecs)


def solution(mesh):
    return jax.shard_map(
        shards,
        mesh=mesh,
        in_specs=(
            P("center", None),
            P("center", None),
            P("dp"),
            P("dp", None),
            P("center", None),
            P("center", None),
            P(),
        ),
        out_specs=P("center", None),
        check_vma=False,
    )
```

time: 110 us -> 80.8 us (0.73)
  Pallas kernels: 106 us -> 79.4 us
  local copies, waits for them, and re-layouts: 4.29 us -> 1.32 us
    pallas_call x1, Pallas kernels: 106 us -> 79.4 us  [shards(): pl.pallas_call(body, out_shape=pltpu.VMEM((ROWS, OUTS), F32), in_specs=[v...]
    unnamed x1, local copies, waits for them, and re-layouts: 3.05 us -> 1.32 us
    pad x1 -> x0, local copies, waits for them, and re-layouts: 1.24 us -> none  [shards(): shr = jnp.pad(shrink, (0, QP - Q)).reshape(1, QP)]
where the time goes in v2:
time: 80.8 us; the launch traced here: 80.7 us
  Pallas kernels  79.4 us (98%)
  local copies, waits for them, and re-layouts  1.32 us (2%)
    pallas_call x1, Pallas kernels, shards(): pl.pallas_call(body, out_shape=pltpu.VMEM((ROWS, OUTS), F32), in_specs=[v...  79.4 us

profile of v2, /device:TPU:1, one launch (start us, length us, event | category | flops | bytes accessed | tf_op | source)
XLA Modules:
  0.0 80.7 jit_solution(5239986511432278331)
XLA Ops:
  0.0 79.4 %eigenpro_step.1 = f32[2048,256]{1,0:T(8,128)S(1)} custom-call(s32[1,256]{1,0:T(1,128)} %bitcast.2, f32[1,200]{1,0:T(1,128)} %bitcast.3, bf16[2048,768]{1,0:T(8,128)(2,1)} %c_hbm.1, f32[2048,256]{1,0:T(8,128)} %w_hbm.1, f32[256,256]{1,0:T(8,128)} %t_hbm.1, bf16[32,768]{1,0:T(8,128)(2,1)} %s_hbm.1, f32[32,200]{1,0:T(8,128)} %e_hbm.1), custom_call_target="tpu_custom_call" | custom-call | tf_op jit(solution)/shard_map/eigenpro_step/pallas_call | solution.py:400
  79.4 1.3 %copy.9 = f32[2048,256]{1,0:T(8,128)} copy(f32[2048,256]{1,0:T(8,128)S(1)} %eigenpro_step.1) | data formatting | bytes 4194304

commit v3 on v2

--- a/solution.py
+++ b/solution.py
@@ -211,7 +211,7 @@
     g_z = {o: remote(own, own, z_peer(o)) for o in FAR_Z}
     g_y = [remote(own, own, y_peer(j)) for j in range(1, NY)]
     recv(s_y)
-    s_x = [remote(sbuf.at[x, :, :, :, lane], sbuf.at[x, :, :, :, lane], x_peer(j)) for j in range(1, NX)]
+    s_x = [remote(sbuf.at[x, :, :, :, lane], sbuf.at[x, :, :, :, lane], x_peer(j)) for j in (1, 3)]
     s_s = [remote(sbuf.at[x, :, :, :, lane], sbuf.at[x, :, :, :, lane], sib)]
     for o in FAR_Z[::-1]:
         recv([g_z[o]])
@@ -264,7 +264,13 @@
     lax.fori_loop(1, NYZ, send_p, 0)
     recv(b_s)
     k_block(dps)
-    drain()
+    recv(s_x)
+    west = sbuf.at[lax.rem(x + 3, NX), :, :, :, lane]
+    east = sbuf.at[lax.rem(x + 1, NX), :, :, :, lane]
+    west_half = sbuf.at[lax.rem(x + 3, NX), pl.ds(0, 2), :, :, lane]
+    east_half = sbuf.at[lax.rem(x + 1, NX), pl.ds(2, 2), :, :, lane]
+    s_f = [remote(west_half, west_half, x_peer(1)), remote(east_half, east_half, x_peer(3))]
+    s_s += [remote(west, west, sib), remote(east, east, sib)]
     recv([b_r, b_l])
     b_s2 = remote(ball.at[dpx], ball.at[dpx], sib)
     k_block(dpx)
@@ -298,6 +304,8 @@
     part_p = lax.fori_loop(1, NYZ, add_p, pred[chunk])
     xsp[...] = part_p
     p_x = remote(xsp, xrp, x_peer(2))
+    recv(s_f)
+    s_s += [remote(sbuf.at[lax.rem(x + 2, NX), :, :, :, lane], sbuf.at[lax.rem(x + 2, NX), :, :, :, lane], sib)]
     recv([p_x])
     rall[dp, chunk] = xsp[...] + xrp[...] - tt[chunk]
 
@@ -308,8 +316,6 @@
         return carry
 
     lax.fori_loop(1, NYZ, send_r, 0)
-    recv(s_x)
-    s_s += [remote(sbuf.at[lax.rem(x + j, NX), :, :, :, lane], sbuf.at[lax.rem(x + j, NX), :, :, :, lane], sib) for j in range(1, NX)]
     recv(e_s + s_s)
     for xx in range(NX):
         s_row[xx] = row_sq(sbuf[xx].reshape(512, D))

time: 80.8 us -> 76.8 us (0.950)
  Pallas kernels: 79.4 us -> 75.4 us
    pallas_call x1, Pallas kernels: 79.4 us -> 75.4 us  [shards(): pl.pallas_call(body, out_shape=pltpu.VMEM((ROWS, OUTS), F32), in_specs=[v...]
where the time goes in v3:
time: 76.8 us; the launch traced here: 76.7 us
  Pallas kernels  75.4 us (98%)
  local copies, waits for them, and re-layouts  1.32 us (2%)
    pallas_call x1, Pallas kernels, shards(): pl.pallas_call(body, out_shape=pltpu.VMEM((ROWS, OUTS), F32), in_specs=[v...  75.4 us

profile of v3, /device:TPU:1, one launch (start us, length us, event | category | flops | bytes accessed | tf_op | source)
XLA Modules:
  0.0 76.7 jit_solution(9623408551194372094)
XLA Ops:
  0.0 75.4 %eigenpro_step.1 = f32[2048,256]{1,0:T(8,128)S(1)} custom-call(s32[1,256]{1,0:T(1,128)} %bitcast.2, f32[1,200]{1,0:T(1,128)} %bitcast.3, bf16[2048,768]{1,0:T(8,128)(2,1)} %c_hbm.1, f32[2048,256]{1,0:T(8,128)} %w_hbm.1, f32[256,256]{1,0:T(8,128)} %t_hbm.1, bf16[32,768]{1,0:T(8,128)(2,1)} %s_hbm.1, f32[32,200]{1,0:T(8,128)} %e_hbm.1), custom_call_target="tpu_custom_call" | custom-call | tf_op jit(solution)/shard_map/eigenpro_step/pallas_call | solution.py:406
  75.4 1.3 %copy.9 = f32[2048,256]{1,0:T(8,128)} copy(f32[2048,256]{1,0:T(8,128)S(1)} %eigenpro_step.1) | data formatting | bytes 4194304

commit v4 on v3

--- a/solution.py
+++ b/solution.py
@@ -101,10 +101,10 @@
         unsent.append(cp)
         return cp
 
-    def drain():
-        for cp in unsent:
+    def drain(count=None):
+        for cp in unsent[:count]:
             cp.wait_send()
-        unsent.clear()
+        del unsent[:count]
 
     def yz_copy(phase, k, src, dst, peer):
         return pltpu.make_async_remote_copy(
@@ -120,6 +120,17 @@
         cp = pltpu.make_async_copy(src, dst, lsem.at[i])
         cp.start()
         return cp
+
+    barrier = pltpu.get_barrier_semaphore()
+
+    def greet(k, carry):
+        pl.semaphore_signal(barrier, inc=1, device_id=yz_peer(NYZ - k)[0], device_id_type=MESH)
+        return carry
+
+    lax.fori_loop(1, NYZ, greet, 0)
+    for j in range(1, NX):
+        pl.semaphore_signal(barrier, inc=1, device_id=x_peer(j), device_id_type=MESH)
+    pl.semaphore_signal(barrier, inc=1, device_id=sib, device_id_type=MESH)
 
     ld_c = local(0, c_hbm, c_v)
     ld_e = local(1, e_hbm, e_v)
@@ -130,17 +141,6 @@
     )
     ld_t = local(3, t_hbm, t_v)
     ld_w = local(4, w_hbm, w_v)
-
-    barrier = pltpu.get_barrier_semaphore()
-
-    def greet(k, carry):
-        pl.semaphore_signal(barrier, inc=1, device_id=yz_peer(k)[0], device_id_type=MESH)
-        return carry
-
-    lax.fori_loop(1, NYZ, greet, 0)
-    for j in range(1, NX):
-        pl.semaphore_signal(barrier, inc=1, device_id=x_peer(j), device_id_type=MESH)
-    pl.semaphore_signal(barrier, inc=1, device_id=sib, device_id_type=MESH)
 
     e_pad[...] = jnp.zeros_like(e_pad)
     ld_e.wait()
@@ -207,6 +207,7 @@
     here = (dp,) + slot(y, z)
     ball[here] = (xsb[...].astype(F32) + xrb[...].astype(F32)).astype(BF)
 
+    early = len(unsent)
     own = ball.at[here]
     g_z = {o: remote(own, own, z_peer(o)) for o in FAR_Z}
     g_y = [remote(own, own, y_peer(j)) for j in range(1, NY)]
@@ -220,10 +221,12 @@
     recv(e_x)
     e_y = [remote(ebuf.at[core, y], ebuf.at[core, y], y_peer(j)) for j in range(1, NY)]
     e_s = [remote(ebuf.at[core, y], ebuf.at[core, y], sib)]
+    drain(early)
     recv(g_y)
     b_s = [remote(ball.at[dp], ball.at[dp], sib)]
     b_r = remote(ball.at[dp, pl.ds(0, 8)], ball.at[dp, pl.ds(0, 8)], x_peer(1))
     b_l = remote(ball.at[dp, pl.ds(8, 8)], ball.at[dp, pl.ds(8, 8)], x_peer(3))
+    batch_sends = len(unsent)
 
     def norms_b(d):
         b_row[d] = row_sq(ball[d].reshape(BD, D))
@@ -276,8 +279,7 @@
     k_block(dpx)
     recv(e_y)
     e_s += [remote(ebuf.at[core, lax.rem(y + j, NY)], ebuf.at[core, lax.rem(y + j, NY)], sib) for j in range(1, NY)]
-    recv([b_s2])
-    k_block(dpxs)
+    drain(batch_sends)
 
     def subset_product(rows_b, left):
         n = rows_b.shape[0]
@@ -304,8 +306,16 @@
     part_p = lax.fori_loop(1, NYZ, add_p, pred[chunk])
     xsp[...] = part_p
     p_x = remote(xsp, xrp, x_peer(2))
+    recv([b_s2])
+    k_block(dpxs)
     recv(s_f)
     s_s += [remote(sbuf.at[lax.rem(x + 2, NX), :, :, :, lane], sbuf.at[lax.rem(x + 2, NX), :, :, :, lane], sib)]
+
+    def sent_p(k, carry):
+        yz_copy(0, k, pred.at[0], rsp.at[0], sib).wait_send()
+        return carry
+
+    lax.fori_loop(1, NYZ, sent_p, 0)
     recv([p_x])
     rall[dp, chunk] = xsp[...] + xrp[...] - tt[chunk]
 
@@ -341,6 +351,12 @@
     g_step(1)
     g_rows = pl.ds(pl.multiple_of(core * 1024, 1024), 1024)
     gm_s = [remote(gbuf.at[:, g_rows], gbuf.at[:, g_rows], sib)]
+
+    def sent_r(k, carry):
+        yz_copy(1, k, rall.at[0, 0], rall.at[0, 0], sib).wait_send()
+        return carry
+
+    lax.fori_loop(1, NYZ, sent_r, 0)
     r_s2 = []
     for j in (0, 1, 3, 2):
         recv([r_x[j]])
@@ -387,13 +403,6 @@
 
     lax.fori_loop(0, ROWS // 256, out_far, 0, unroll=True)
     drain()
-
-    def sent(k, carry):
-        yz_copy(0, k, pred.at[0], rsp.at[0], sib).wait_send()
-        yz_copy(1, k, rall.at[0, 0], rall.at[0, 0], sib).wait_send()
-        return carry
-
-    lax.fori_loop(1, NYZ, sent, 0)
 
 
 N_MISC = 144

time: 76.8 us -> 74.3 us (0.967)
  Pallas kernels: 75.4 us -> 72.9 us
    pallas_call x1, Pallas kernels: 75.4 us -> 72.9 us  [shards(): pl.pallas_call(body, out_shape=pltpu.VMEM((ROWS, OUTS), F32), in_specs=[v...]
where the time goes in v4:
time: 74.3 us; the launch traced here: 74.2 us
  Pallas kernels  72.9 us (98%)
  local copies, waits for them, and re-layouts  1.32 us (2%)
    pallas_call x1, Pallas kernels, shards(): pl.pallas_call(body, out_shape=pltpu.VMEM((ROWS, OUTS), F32), in_specs=[v...  72.9 us

profile of v4, /device:TPU:1, one launch (start us, length us, event | category | flops | bytes accessed | tf_op | source)
XLA Modules:
  0.0 74.2 jit_solution(10927999790323006027)
XLA Ops:
  0.0 72.9 %eigenpro_step.1 = f32[2048,256]{1,0:T(8,128)S(1)} custom-call(s32[1,256]{1,0:T(1,128)} %bitcast.2, f32[1,200]{1,0:T(1,128)} %bitcast.3, bf16[2048,768]{1,0:T(8,128)(2,1)} %c_hbm.1, f32[2048,256]{1,0:T(8,128)} %w_hbm.1, f32[256,256]{1,0:T(8,128)} %t_hbm.1, bf16[32,768]{1,0:T(8,128)(2,1)} %s_hbm.1, f32[32,200]{1,0:T(8,128)} %e_hbm.1), custom_call_target="tpu_custom_call" | custom-call | tf_op jit(solution)/shard_map/eigenpro_step/pallas_call | solution.py:415
  72.9 1.3 %copy.9 = f32[2048,256]{1,0:T(8,128)} copy(f32[2048,256]{1,0:T(8,128)S(1)} %eigenpro_step.1) | data formatting | bytes 4194304
